TPU v7x, 32 devices: a whole 2x2x4 slice. The times are simulated.
32 devices in a mesh: tm: 4 (over z), ha: 2 (over y), wa: 4 (over x, core).
Axes of the slice: x: 2, y: 2, z: 4, core: 2. Of those that a mesh axis runs over, the one named last changes fastest.
Arguments:
- latent: bfloat16 [8, 32, 64, 512], P('tm', 'ha', 'wa'), may hold values from -1300 to 1300
- norm_gain: float32 [512], replicated, may hold values from 0.1 to 1.9
- norm_bias: float32 [512], replicated, may hold values from -3 to 3
- conv_weight: bfloat16 [3, 3, 3, 512, 256], replicated, may hold values from -0.0546875 to 0.0546875
- conv_bias: float32 [256], replicated, may hold values from -3 to 3
- up_weight: bfloat16 [4, 4, 256, 256], replicated, may hold values from -0.1875 to 0.1875
- up_bias: float32 [256], replicated, may hold values from -3 to 3
Outputs:
- video: bfloat16 [8, 64, 128, 256], P('tm', 'ha', 'wa')
All inputs are finite; a program needn't handle non-finite values.
Results may differ from a plain program's by a relative error of at most 0.0054.
Values may be sent and summed in bfloat16 or wider, within the bound.
A program may use at most 64 MiB of HBM per device.

v0:
```python
import jax
import jax.numpy as jnp
from jax import lax
from jax.sharding import PartitionSpec as P

GROUPS = 32


def prefix(part, axis, combine, identity):
    place = lax.axis_index(axis)
    gathered = jax.tree.map(lambda a: lax.all_gather(a, axis), part)
    state = jax.tree.map(lambda a, e: jnp.zeros_like(a) + jnp.asarray(e, a.dtype), part, identity)

    def one(hop, state):
        return combine(
            state, jax.tree.map(lambda a: lax.dynamic_index_in_dim(a, hop, 0, False), gathered)
        )

    return lax.fori_loop(0, place, one, state)


def padded_2(block, sides, width):
    for axis, dim in sides:
        count = lax.axis_size(axis)
        forward = [(i, i + 1) for i in range(count - 1)]
        backward = [(target, source) for source, target in forward]
        low = lax.ppermute(
            lax.slice_in_dim(block, block.shape[dim] - width, None, axis=dim), axis, forward
        )
        high = lax.ppermute(lax.slice_in_dim(block, 0, width, axis=dim), axis, backward)
        block = jnp.concatenate([low, block, high], axis=dim)
    return block


def from_behind(array, axis, by):
    devices = lax.axis_size(axis)
    pairs = [(i, i + by) for i in range(devices) if 0 <= i + by < devices]
    return lax.ppermute(array, axis, pairs)


def group_totals(latent):
    wide = latent.astype(jnp.float32)
    sums = jnp.sum(wide, axis=(0, 1, 2)).reshape(GROUPS, -1).sum(axis=1)
    squares = jnp.sum(wide * wide, axis=(0, 1, 2)).reshape(GROUPS, -1).sum(axis=1)
    return (sums, squares)


def add_pair(earlier, later):
    return (earlier[0] + later[0], earlier[1] + later[1])


def tap_sum(source, weights, height, breadth):
    count = source.shape[0]
    summed = None
    for row_tap in range(3):
        joined = jnp.concatenate(
            [
                source[:, row_tap : row_tap + height, col_tap : col_tap + breadth, :]
                for col_tap in range(3)
            ],
            axis=-1,
        )
        joined = joined.reshape(count * height * breadth, -1)
        term = jnp.dot(
            joined,
            weights[row_tap].reshape(-1, weights.shape[-1]),
            preferred_element_type=jnp.float32,
        )
        summed = term if summed is None else summed + term
    return summed


def upsample_tile(values, up_weight):
    frames, height, breadth, chans = values.shape
    flat = values.reshape(frames * height * breadth, chans)
    rows_out = []
    for row_par in (0, 1):
        cols_out = []
        for col_par in (0, 1):
            joined = jnp.concatenate(
                [
                    up_weight[row_par + 2 * shift_row, col_par + 2 * shift_col]
                    for shift_row in (0, 1)
                    for shift_col in (0, 1)
                ],
                axis=1,
            )
            product = jnp.dot(flat, joined, preferred_element_type=jnp.float32).reshape(
                frames, height, breadth, 4, chans
            )
            summed = jnp.zeros((frames, height + 1, breadth + 1, chans), jnp.float32)
            for shift_row in (0, 1):
                for shift_col in (0, 1):
                    summed = summed + jnp.pad(
                        product[:, :, :, 2 * shift_row + shift_col],
                        ((0, 0), (shift_row, 1 - shift_row), (shift_col, 1 - shift_col), (0, 0)),
                    )
            cols_out.append(summed)
        rows_out.append(jnp.stack(cols_out, axis=3))
    return jnp.stack(rows_out, axis=2).reshape(frames, 2 * height + 2, 2 * breadth + 2, chans)


def shards(latent, norm_gain, norm_bias, conv_weight, conv_bias, up_weight, up_bias):
    frames, height, breadth, channels = latent.shape
    block_index = lax.axis_index("tm")
    tile_sums, tile_squares = group_totals(latent)
    block_sums, block_squares = lax.psum((tile_sums, tile_squares), ("ha", "wa"))
    zeros_pair = (jnp.zeros_like(block_sums), jnp.zeros_like(block_squares))
    before = prefix((block_sums, block_squares), "tm", add_pair, zeros_pair)
    upto_sums = before[0] + block_sums
    upto_squares = before[1] + block_squares
    group_width = channels // GROUPS
    cells = float(
        frames * height * breadth * lax.axis_size("ha") * lax.axis_size("wa") * group_width
    )
    counted = (block_index + 1).astype(jnp.float32) * cells
    mean = upto_sums / counted
    variance = upto_squares / counted - mean * mean
    inverse = lax.rsqrt(variance + 1e-06)
    mean_chan = jnp.repeat(mean, group_width)
    inverse_chan = jnp.repeat(inverse, group_width)
    normed = jax.nn.silu(
        (latent.astype(jnp.float32) - mean_chan) * inverse_chan * norm_gain + norm_bias
    ).astype(jnp.bfloat16)
    padded = padded_2(normed, (("ha", 1), ("wa", 2)), 1)
    earlier = from_behind(padded, "tm", 1)
    opening = jnp.stack([padded[0], padded[0]])
    earlier = jnp.where(block_index == 0, opening, earlier)
    extended = jnp.concatenate([earlier, padded], axis=0)
    summed = None
    for lag_step in range(3):
        term = tap_sum(
            extended[lag_step : lag_step + frames], conv_weight[lag_step], height, breadth
        )
        summed = term if summed is None else summed + term
    features = (summed + conv_bias).astype(jnp.bfloat16).reshape(frames, height, breadth, -1)
    spread = upsample_tile(features, up_weight)
    from_above = from_behind(spread[:, -1].astype(jnp.bfloat16), "ha", 1).astype(jnp.float32)
    from_below = from_behind(spread[:, 0].astype(jnp.bfloat16), "ha", -1).astype(jnp.float32)
    middle = spread[:, 1:-1]
    middle = middle.at[:, 0].add(from_above)
    middle = middle.at[:, -1].add(from_below)
    from_left = from_behind(middle[:, :, -1].astype(jnp.bfloat16), "wa", 1).astype(jnp.float32)
    from_right = from_behind(middle[:, :, 0].astype(jnp.bfloat16), "wa", -1).astype(jnp.float32)
    inner = middle[:, :, 1:-1]
    inner = inner.at[:, :, 0].add(from_left)
    inner = inner.at[:, :, -1].add(from_right)
    return (inner + up_bias).astype(jnp.bfloat16)


def solution(mesh):
    in_specs = (P("tm", "ha", "wa", None), P(), P(), P(), P(), P(), P())
    out_specs = P("tm", "ha", "wa", None)
    return jax.shard_map(shards, mesh=mesh, in_specs=in_specs, out_specs=out_specs, check_vma=False)
```

profile of v0, /device:TPU:17, one launch (start us, length us, event | category | flops | bytes accessed | tf_op | source)
XLA Modules:
  0.0 142.2 jit_solution(13787219909280827165)
XLA Ops:
  0.0 1.2 fusion.9
  1.6 11.8 %all-reduce.18 = (f32[32]{0:T(128)S(1)}, f32[32]{0:T(128)S(1)}) all-reduce(f32[32]{0:T(128)S(1)} %reduce_sum.37, f32[32]{0:T(128)S(1)} %reduce_sum.39), channel_id=1, replica_groups=mesh['tm'=4,'ha'=2,'wa'=4] {'ha','wa'}, use_global_device_ids=true, to_apply=%region_2.0 | all-reduce | flops 64 | bytes 512 | tf_op jit(solution)/shard_map/psum | solution.py:107
  13.4 1.2 dynamic-slice.32
  15.7 7.1 %all-reduce.19 = (f32[128]{0:T(128)S(1)}, f32[128]{0:T(128)S(1)}) all-reduce(f32[128]{0:T(128)S(1)} %dynamic-update-slice.12, f32[128]{0:T(128)S(1)} %dynamic-update-slice.13), channel_id=2, replica_groups=mesh['tm'=4,'ha'=2,'wa'=4] {'tm'}, use_global_device_ids=true, to_apply=%add.16 | all-reduce | flops 256 | bytes 2048
  23.3 1.4 %fusion.18 = bf16[2,16,16,512]{3,2,1,0:T(8,128)(2,1)S(1)} fusion(bf16[2,16,16,512]{3,2,1,0:T(8,128)(2,1)} %param.17, f32[512]{0:T(512)} %param.19, f32[512]{0:T(512)} %param.18, f32[512]{0:T(512)S(1)} %mul.34, f32[512]{0:T(512)S(1)} %sub.13), kind=kLoop, calls=%fused_computation.42 | loop fusion | flops 2621440 | bytes 1056768 | tf_op jit(solution)/shard_map/convert_element_type | solution.py:124
  24.8 1.3 collective-permute-start.1
  26.1 4.0 %collective-permute-start = (bf16[2,1,16,512]{3,2,1,0:T(8,128)(2,1)S(1)}, bf16[2,1,16,512]{3,2,1,0:T(8,128)(2,1)S(1)}, u32[]{:S(2)}, u32[]{:S(2)}) collective-permute-start(bf16[2,1,16,512]{3,2,1,0:T(8,128)(2,1)S(1)} %get-tuple-element.187), channel_id=1, source_target_pairs={{0,4},{1,5},{2,6},{3,7},{8,12},{9,13},{10,14},{11,15},{16,20},{17,... | collective-permute-start | bytes 98312 | tf_op jit(solution)/shard_map/ppermute | solution.py:27
  30.1 5.9 %fusion.58 = (bf16[1,1,3,512,256]{4,3,2,1,0:T(8,128)(2,1)S(1)}, bf16[1,1,3,512,256]{4,3,2,1,0:T(8,128)(2,1)}, bf16[1,1,3,512,256]{4,3,2,1,0:T(8,128)(2,1)}, bf16...) fusion(bf16[3,3,3,512,256]{4,3,2,1,0:T(8,128)(2,1)} %param.20), kind=kLoop, calls=%fused_computation.136 | loop fusion | bytes 14155776 | tf_op jit(solution)/shard_map/slice | solution.py:66
  36.1 6.9 %collective-permute-start.3 = (bf16[2,18,1,512]{3,2,1,0:T(2,128)(2,1)S(1)}, bf16[2,18,1,512]{3,2,1,0:T(2,128)(2,1)S(1)}, u32[]{:S(2)}, u32[]{:S(2)}) collective-permute-start(bf16[2,18,1,512]{3,2,1,0:T(2,128)(2,1)S(1)} %get-tuple-element.183), channel_id=1, source_target_pairs={{1,0},{2,1},{3,2},{5,4},{6,5},{7,6},{9,8},{10,9},{11,10},{13,12},{... | collective-permute-start | bytes 110600 | tf_op jit(solution)/shard_map/ppermute | solution.py:30
  43.0 1.9 %collective-permute-start.2 = (bf16[2,18,1,512]{3,2,1,0:T(2,128)(2,1)S(1)}, bf16[2,18,1,512]{3,2,1,0:T(2,128)(2,1)S(1)}, u32[]{:S(2)}, u32[]{:S(2)}) collective-permute-start(bf16[2,18,1,512]{3,2,1,0:T(2,128)(2,1)S(1)} %get-tuple-element.182), channel_id=1, source_target_pairs={{0,1},{1,2},{2,3},{4,5},{5,6},{6,7},{8,9},{9,10},{10,11},{12,13},{... | collective-permute-start | bytes 110600 | tf_op jit(solution)/shard_map/ppermute | solution.py:27
  45.0 1.2 slice_bitcast_fusion.15
  46.9 2.4 %collective-permute-start.4 = (bf16[2,18,18,512]{3,2,1,0:T(8,128)(2,1)S(1)}, bf16[2,18,18,512]{3,2,1,0:T(8,128)(2,1)S(1)}, u32[]{:S(2)}, u32[]{:S(2)}) collective-permute-start(bf16[2,18,18,512]{3,2,1,0:T(8,128)(2,1)S(1)} %pad_maximum_fusion.10), channel_id=1, source_target_pairs={{0,8},{8,16},{16,24},{1,9},{9,17},{17,25},{2,10},{10,18},{18,26},{... | collective-permute-start | bytes 1990664 | tf_op jit(solution)/shard_map/ppermute | solution.py:38
  52.5 17.2 %collective-permute-done.4 = bf16[2,18,18,512]{3,2,1,0:T(8,128)(2,1)S(1)} collective-permute-done((bf16[2,18,18,512]{3,2,1,0:T(8,128)(2,1)S(1)}, bf16[2,18,18,512]{3,2,1,0:T(8,128)(2,1)S(1)}, u32[]{:S(2)}, u32[]{:S(2)}) %collective-permute-start.4) | collective-permute-done | bytes 663584 | tf_op jit(solution)/shard_map/ppermute | solution.py:38
  72.0 0.8 copy-done.1
  73.8 0.8 copy-done
  75.9 1.0 copy-done.6
  78.2 1.0 copy-done.4
  80.9 1.8 %fusion.43 = f32[512,1024]{1,0:T(8,128)} fusion(bf16[512,256]{1,0:T(8,128)(2,1)S(1)} %fusion.8, bf16[256,256]{1,0:T(8,128)(2,1)S(1)} %copy-done.30, bf16[256,256]{1,0:T(8,128)(2,1)S(1)} %copy-done.31, bf16[256,256]{1,0:T(8,128)(2,1)S(1)} %get-tuple-element.125, bf16[256,256]{1,0:T(8,128)(2,1)S(1)} %get-tuple-element.126), kind=kOutput, calls=%fused_computation.75 | convolution fusion | flops 270532608 | bytes 2883584 | tf_op jit(solution)/shard_map/dot_general | solution.py:88
  82.6 2.2 %reshape.235 = f32[2,16,16,4,256]{4,3,2,1,0:T(4,128)S(1)} reshape(f32[512,1024]{1,0:T(8,128)} %fusion.43) | data formatting | bytes 4194304 | tf_op jit(solution)/shard_map/reshape | solution.py:88
  84.8 1.9 %fusion.62 = (f32[2,16,16,1,256]{4,3,2,1,0:T(1,128)S(1)}, f32[2,16,16,1,256]{4,3,2,1,0:T(1,128)S(1)}, f32[2,16,16,1,256]{4,3,2,1,0:T(1,128)S(1)}, f32[2,16,16,1,256]{4,3,2,1,0:T(1,128)S(1)}) fusion(f32[2,16,16,4,256]{4,3,2,1,0:T(4,128)S(1)} %reshape.235), kind=kLoop, calls=%fused_computation.140 | loop fusion | bytes 4194304 | tf_op jit(solution)/shard_map/slice | solution.py:95
  86.9 0.8 copy.82
  87.7 0.8 copy.83
  88.6 1.8 %fusion.35 = f32[512,1024]{1,0:T(8,128)} fusion(bf16[512,256]{1,0:T(8,128)(2,1)S(1)} %fusion.8, bf16[256,256]{1,0:T(8,128)(2,1)S(1)} %copy-done.26, bf16[256,256]{1,0:T(8,128)(2,1)S(1)} %copy-done.27, bf16[256,256]{1,0:T(8,128)(2,1)S(1)} %copy-done.28, bf16[256,256]{1,0:T(8,128)(2,1)S(1)} %copy-done.29), kind=kOutput, calls=%fused_computation.67 | convolution fusion | flops 270532608 | bytes 2883584 | tf_op jit(solution)/shard_map/dot_general | solution.py:88
  90.4 2.2 %reshape.234 = f32[2,16,16,4,256]{4,3,2,1,0:T(4,128)S(1)} reshape(f32[512,1024]{1,0:T(8,128)} %fusion.35) | data formatting | bytes 4194304 | tf_op jit(solution)/shard_map/reshape | solution.py:88
  92.6 1.9 %fusion.61 = (f32[2,16,16,1,256]{4,3,2,1,0:T(1,128)S(1)}, f32[2,16,16,1,256]{4,3,2,1,0:T(1,128)S(1)}, f32[2,16,16,1,256]{4,3,2,1,0:T(1,128)S(1)}, f32[2,16,16,1,256]{4,3,2,1,0:T(1,128)S(1)}) fusion(f32[2,16,16,4,256]{4,3,2,1,0:T(4,128)S(1)} %reshape.234), kind=kLoop, calls=%fused_computation.139 | loop fusion | bytes 4194304 | tf_op jit(solution)/shard_map/slice | solution.py:95
  94.5 0.8 copy.84
  95.3 0.8 copy.85
  96.2 0.8 copy.86
  97.0 0.8 copy.87
  97.9 1.8 %fusion.27 = f32[512,1024]{1,0:T(8,128)} fusion(bf16[512,256]{1,0:T(8,128)(2,1)S(1)} %fusion.8, bf16[256,256]{1,0:T(8,128)(2,1)S(1)} %copy-done.22, bf16[256,256]{1,0:T(8,128)(2,1)S(1)} %copy-done.23, bf16[256,256]{1,0:T(8,128)(2,1)S(1)} %copy-done.24, bf16[256,256]{1,0:T(8,128)(2,1)S(1)} %copy-done.25), kind=kOutput, calls=%fused_computation.59 | convolution fusion | flops 270532608 | bytes 2883584 | tf_op jit(solution)/shard_map/dot_general | solution.py:88
  99.7 2.2 %reshape.233 = f32[2,16,16,4,256]{4,3,2,1,0:T(4,128)S(1)} reshape(f32[512,1024]{1,0:T(8,128)} %fusion.27) | data formatting | bytes 4194304 | tf_op jit(solution)/shard_map/reshape | solution.py:88
  101.9 1.9 %fusion.60 = (f32[2,16,16,1,256]{4,3,2,1,0:T(1,128)S(1)}, f32[2,16,16,1,256]{4,3,2,1,0:T(1,128)S(1)}, f32[2,16,16,1,256]{4,3,2,1,0:T(1,128)S(1)}, f32[2,16,16,1,256]{4,3,2,1,0:T(1,128)S(1)}) fusion(f32[2,16,16,4,256]{4,3,2,1,0:T(4,128)S(1)} %reshape.233), kind=kLoop, calls=%fused_computation.138 | loop fusion | bytes 4194304 | tf_op jit(solution)/shard_map/slice | solution.py:95
  103.8 0.9 copy.88
  104.7 0.9 copy.89
  105.5 0.8 copy.90
  107.6 2.0 %reshape.232 = f32[2,16,16,4,256]{4,3,2,1,0:T(4,128)} reshape(f32[512,1024]{1,0:T(8,128)S(1)} %fusion.19) | data formatting | bytes 4194304 | tf_op jit(solution)/shard_map/reshape | solution.py:88
  109.7 5.9 %fusion.59 = (f32[2,16,16,1,256]{4,3,2,1,0:T(1,128)S(1)}, f32[2,16,16,1,256]{4,3,2,1,0:T(1,128)S(1)}, f32[2,16,16,1,256]{4,3,2,1,0:T(1,128)S(1)}, f32[2,16,16,1,256]{4,3,2,1,0:T(1,128)S(1)}) fusion(f32[2,16,16,4,256]{4,3,2,1,0:T(4,128)} %reshape.232), kind=kLoop, calls=%fused_computation.137 | loop fusion | bytes 4194304 | tf_op jit(solution)/shard_map/slice | solution.py:95
  115.8 0.9 copy-done.9
  117.9 0.9 copy-done.15
  120.3 1.2 copy.43
  122.4 1.3 collective-permute-start.5
  124.5 1.3 collective-permute-start.6
  126.3 2.9 %collective-permute-done.6 = bf16[2,34,256]{2,0,1:T(2,128)(2,1)S(1)} collective-permute-done((bf16[2,34,256]{2,0,1:T(2,128)(2,1)S(1)}, bf16[2,34,256]{2,0,1:T(2,128)(2,1)S(1)}, u32[]{:S(2)}, u32[]{:S(2)}) %collective-permute-start.6) | collective-permute-done | bytes 34848 | tf_op jit(solution)/shard_map/ppermute | solution.py:38
  129.3 2.8 %scatter-add.15 = f32[2,32,34,256]{3,1,0,2:T(8,128)S(1)} dynamic-update-slice(f32[2,32,34,256]{3,1,0,2:T(8,128)S(1)} %copy.45, f32[2,1,34,256]{3,1,0,2:T(1,128)S(1)} %copy_add_fusion, s32[]{:T(128)} %constant.128.clone.1, s32[]{:T(128)} %constant.134.clone.1, s32[]{:T(128)} %constant.128.clone.1, s32[]{:T(128)} %constant.128.clone.1) | dynamic-update-slice | bytes 139268 | tf_op jit(solution)/shard_map/scatter-add | solution.py:142
  132.4 2.5 %collective-permute-start.7 = (bf16[2,32,256]{2,1,0:T(8,128)(2,1)S(1)}, bf16[2,32,256]{2,1,0:T(8,128)(2,1)S(1)}, u32[]{:S(2)}, u32[]{:S(2)}) collective-permute-start(bf16[2,32,256]{2,1,0:T(8,128)(2,1)S(1)} %get-tuple-element.164), channel_id=1, source_target_pairs={{0,1},{1,2},{2,3},{4,5},{5,6},{6,7},{8,9},{9,10},{10,11},{12,13},{... | collective-permute-start | bytes 98312 | tf_op jit(solution)/shard_map/ppermute | solution.py:38
  135.0 3.0 %collective-permute-start.8 = (bf16[2,32,256]{2,1,0:T(8,128)(2,1)S(1)}, bf16[2,32,256]{2,1,0:T(8,128)(2,1)S(1)}, u32[]{:S(2)}, u32[]{:S(2)}) collective-permute-start(bf16[2,32,256]{2,1,0:T(8,128)(2,1)S(1)} %get-tuple-element.163), channel_id=1, source_target_pairs={{1,0},{2,1},{3,2},{5,4},{6,5},{7,6},{9,8},{10,9},{11,10},{13,12},{... | collective-permute-start | bytes 98312 | tf_op jit(solution)/shard_map/ppermute | solution.py:38
  138.1 2.2 %collective-permute-done.8 = bf16[2,32,256]{2,1,0:T(8,128)(2,1)S(1)} collective-permute-done((bf16[2,32,256]{2,1,0:T(8,128)(2,1)S(1)}, bf16[2,32,256]{2,1,0:T(8,128)(2,1)S(1)}, u32[]{:S(2)}, u32[]{:S(2)}) %collective-permute-start.8) | collective-permute-done | bytes 32800 | tf_op jit(solution)/shard_map/ppermute | solution.py:38
  140.6 1.6 %copy.46 = bf16[2,32,32,256]{3,2,1,0:T(8,128)(2,1)} copy(bf16[2,32,32,256]{3,1,0,2:T(8,128)(2,1)S(1)} %add_convert_fusion) | data formatting | bytes 2097152 | tf_op jit(solution)/shard_map/convert_element_type | solution.py:148
  (141 shorter events, 19.9 us)
Async XLA Ops:
  24.8 11.3 %collective-permute-start.1 = (bf16[2,1,16,512]{3,2,1,0:T(8,128)(2,1)S(1)}, bf16[2,1,16,512]{3,2,1,0:T(8,128)(2,1)S(1)}, u32[]{:S(2)}, u32[]{:S(2)}) collective-permute-start(bf16[2,1,16,512]{3,2,1,0:T(8,128)(2,1)S(1)} %get-tuple-element.188), channel_id=1, source_target_pairs={{4,0},{5,1},{6,2},{7,3},{12,8},{13,9},{14,10},{15,11},{20,16},{21,... | collective-permute-start | bytes 98312 | tf_op jit(solution)/shard_map/ppermute | solution.py:30
  26.1 10.0 %collective-permute-start = (bf16[2,1,16,512]{3,2,1,0:T(8,128)(2,1)S(1)}, bf16[2,1,16,512]{3,2,1,0:T(8,128)(2,1)S(1)}, u32[]{:S(2)}, u32[]{:S(2)}) collective-permute-start(bf16[2,1,16,512]{3,2,1,0:T(8,128)(2,1)S(1)} %get-tuple-element.187), channel_id=1, source_target_pairs={{0,4},{1,5},{2,6},{3,7},{8,12},{9,13},{10,14},{11,15},{16,20},{17,... | collective-permute-start | bytes 98312 | tf_op jit(solution)/shard_map/ppermute | solution.py:27
  30.1 14.9 %copy-start.8 = (bf16[4,4,256,256]{3,2,1,0:T(8,128)(2,1)S(1)}, bf16[4,4,256,256]{3,2,1,0:T(8,128)(2,1)}, u32[]{:S(2)}) copy-start(bf16[4,4,256,256]{3,2,1,0:T(8,128)(2,1)} %param.22) | copy-start | bytes 6291460
  36.1 10.0 %collective-permute-start.3 = (bf16[2,18,1,512]{3,2,1,0:T(2,128)(2,1)S(1)}, bf16[2,18,1,512]{3,2,1,0:T(2,128)(2,1)S(1)}, u32[]{:S(2)}, u32[]{:S(2)}) collective-permute-start(bf16[2,18,1,512]{3,2,1,0:T(2,128)(2,1)S(1)} %get-tuple-element.183), channel_id=1, source_target_pairs={{1,0},{2,1},{3,2},{5,4},{6,5},{7,6},{9,8},{10,9},{11,10},{13,12},{... | collective-permute-start | bytes 110600 | tf_op jit(solution)/shard_map/ppermute | solution.py:30
  43.0 3.3 %collective-permute-start.2 = (bf16[2,18,1,512]{3,2,1,0:T(2,128)(2,1)S(1)}, bf16[2,18,1,512]{3,2,1,0:T(2,128)(2,1)S(1)}, u32[]{:S(2)}, u32[]{:S(2)}) collective-permute-start(bf16[2,18,1,512]{3,2,1,0:T(2,128)(2,1)S(1)} %get-tuple-element.182), channel_id=1, source_target_pairs={{0,1},{1,2},{2,3},{4,5},{5,6},{6,7},{8,9},{9,10},{10,11},{12,13},{... | collective-permute-start | bytes 110600 | tf_op jit(solution)/shard_map/ppermute | solution.py:27
  46.9 22.8 %collective-permute-start.4 = (bf16[2,18,18,512]{3,2,1,0:T(8,128)(2,1)S(1)}, bf16[2,18,18,512]{3,2,1,0:T(8,128)(2,1)S(1)}, u32[]{:S(2)}, u32[]{:S(2)}) collective-permute-start(bf16[2,18,18,512]{3,2,1,0:T(8,128)(2,1)S(1)} %pad_maximum_fusion.10), channel_id=1, source_target_pairs={{0,8},{8,16},{16,24},{1,9},{9,17},{17,25},{2,10},{10,18},{18,26},{... | collective-permute-start | bytes 1990664 | tf_op jit(solution)/shard_map/ppermute | solution.py:38
  50.2 1.1 copy-start.3
  50.7 1.2 copy-start.2
  71.8 1.1 copy-start.1
  73.5 1.1 copy-start
  73.8 1.4 copy-start.7
  75.8 1.1 copy-start.6
  75.9 1.6 %copy-start.5 = (bf16[1,1,3,512,256]{4,3,2,1,0:T(8,128)(2,1)S(1)}, bf16[1,1,3,512,256]{4,3,2,1,0:T(8,128)(2,1)}, u32[]{:S(2)}) copy-start(bf16[1,1,3,512,256]{4,3,2,1,0:T(8,128)(2,1)} %get-tuple-element.114) | copy-start | bytes 2359300
  78.1 1.1 copy-start.4
  79.2 0.7 copy-start.32
  79.9 0.9 copy-start.30
  79.9 1.0 copy-start.31
  86.8 1.8 %copy-start.26 = (bf16[256,256]{1,0:T(8,128)(2,1)S(1)}, bf16[256,256]{1,0:T(8,128)(2,1)}, u32[]{:S(2)}) copy-start(bf16[256,256]{1,0:T(8,128)(2,1)} %get-tuple-element.127) | copy-start | bytes 393220
  86.8 1.8 %copy-start.27 = (bf16[256,256]{1,0:T(8,128)(2,1)S(1)}, bf16[256,256]{1,0:T(8,128)(2,1)}, u32[]{:S(2)}) copy-start(bf16[256,256]{1,0:T(8,128)(2,1)} %get-tuple-element.128) | copy-start | bytes 393220
  86.8 1.7 %copy-start.28 = (bf16[256,256]{1,0:T(8,128)(2,1)S(1)}, bf16[256,256]{1,0:T(8,128)(2,1)}, u32[]{:S(2)}) copy-start(bf16[256,256]{1,0:T(8,128)(2,1)} %get-tuple-element.129) | copy-start | bytes 393220
  86.8 1.7 %copy-start.29 = (bf16[256,256]{1,0:T(8,128)(2,1)S(1)}, bf16[256,256]{1,0:T(8,128)(2,1)}, u32[]{:S(2)}) copy-start(bf16[256,256]{1,0:T(8,128)(2,1)} %get-tuple-element.130) | copy-start | bytes 393220
  95.3 2.5 %copy-start.22 = (bf16[256,256]{1,0:T(8,128)(2,1)S(1)}, bf16[256,256]{1,0:T(8,128)(2,1)}, u32[]{:S(2)}) copy-start(bf16[256,256]{1,0:T(8,128)(2,1)} %get-tuple-element.131) | copy-start | bytes 393220
  95.3 2.5 %copy-start.23 = (bf16[256,256]{1,0:T(8,128)(2,1)S(1)}, bf16[256,256]{1,0:T(8,128)(2,1)}, u32[]{:S(2)}) copy-start(bf16[256,256]{1,0:T(8,128)(2,1)} %get-tuple-element.132) | copy-start | bytes 393220
  95.3 2.5 %copy-start.24 = (bf16[256,256]{1,0:T(8,128)(2,1)S(1)}, bf16[256,256]{1,0:T(8,128)(2,1)}, u32[]{:S(2)}) copy-start(bf16[256,256]{1,0:T(8,128)(2,1)} %get-tuple-element.133) | copy-start | bytes 393220
  95.3 2.5 %copy-start.25 = (bf16[256,256]{1,0:T(8,128)(2,1)S(1)}, bf16[256,256]{1,0:T(8,128)(2,1)}, u32[]{:S(2)}) copy-start(bf16[256,256]{1,0:T(8,128)(2,1)} %get-tuple-element.134) | copy-start | bytes 393220
  104.7 2.5 %copy-start.19 = (bf16[256,256]{1,0:T(8,128)(2,1)S(1)}, bf16[256,256]{1,0:T(8,128)(2,1)}, u32[]{:S(2)}) copy-start(bf16[256,256]{1,0:T(8,128)(2,1)} %get-tuple-element.135) | copy-start | bytes 393220
  104.7 2.5 %copy-start.20 = (bf16[256,256]{1,0:T(8,128)(2,1)S(1)}, bf16[256,256]{1,0:T(8,128)(2,1)}, u32[]{:S(2)}) copy-start(bf16[256,256]{1,0:T(8,128)(2,1)} %get-tuple-element.136) | copy-start | bytes 393220
  104.7 2.5 %copy-start.21 = (bf16[256,256]{1,0:T(8,128)(2,1)S(1)}, bf16[256,256]{1,0:T(8,128)(2,1)}, u32[]{:S(2)}) copy-start(bf16[256,256]{1,0:T(8,128)(2,1)} %get-tuple-element.137) | copy-start | bytes 393220
  115.6 1.0 copy-start.9
  115.6 1.2 copy-start.10
  115.7 1.4 copy-start.11
  115.7 1.4 %copy-start.12 = (f32[2,16,16,1,256]{4,2,1,0,3:T(8,128)S(1)}, f32[2,16,16,1,256]{4,2,1,0,3:T(8,128)}, u32[]{:S(2)}) copy-start(f32[2,16,16,1,256]{4,2,1,0,3:T(8,128)} %copy.85) | copy-start | bytes 1572868
  115.7 1.6 %copy-start.13 = (f32[2,16,16,1,256]{4,2,1,0,3:T(8,128)S(1)}, f32[2,16,16,1,256]{4,2,1,0,3:T(8,128)}, u32[]{:S(2)}) copy-start(f32[2,16,16,1,256]{4,2,1,0,3:T(8,128)} %copy.86) | copy-start | bytes 1572868
  115.7 1.7 %copy-start.14 = (f32[2,16,16,1,256]{4,2,1,0,3:T(8,128)S(1)}, f32[2,16,16,1,256]{4,2,1,0,3:T(8,128)}, u32[]{:S(2)}) copy-start(f32[2,16,16,1,256]{4,2,1,0,3:T(8,128)} %copy.87) | copy-start | bytes 1572868
  117.7 1.0 copy-start.15
  117.7 1.2 copy-start.16
  117.8 1.3 copy-start.17
  117.8 1.5 %copy-start.18 = (f32[2,16,16,1,256]{4,2,1,0,3:T(8,128)S(1)}, f32[2,16,16,1,256]{4,2,1,0,3:T(8,128)}, u32[]{:S(2)}) copy-start(f32[2,16,16,1,256]{4,2,1,0,3:T(8,128)} %copy.91) | copy-start | bytes 1572868
  122.4 3.4 %collective-permute-start.5 = (bf16[2,34,256]{2,0,1:T(2,128)(2,1)S(1)}, bf16[2,34,256]{2,0,1:T(2,128)(2,1)S(1)}, u32[]{:S(2)}, u32[]{:S(2)}) collective-permute-start(bf16[2,34,256]{2,0,1:T(2,128)(2,1)S(1)} %get-tuple-element.162), channel_id=1, source_target_pairs={{0,4},{1,5},{2,6},{3,7},{8,12},{9,13},{10,14},{11,15},{16,20},{17,... | collective-permute-start | bytes 104456 | tf_op jit(solution)/shard_map/ppermute | solution.py:38
  124.5 4.7 %collective-permute-start.6 = (bf16[2,34,256]{2,0,1:T(2,128)(2,1)S(1)}, bf16[2,34,256]{2,0,1:T(2,128)(2,1)S(1)}, u32[]{:S(2)}, u32[]{:S(2)}) collective-permute-start(bf16[2,34,256]{2,0,1:T(2,128)(2,1)S(1)} %get-tuple-element.161), channel_id=1, source_target_pairs={{4,0},{5,1},{6,2},{7,3},{12,8},{13,9},{14,10},{15,11},{20,16},{21,... | collective-permute-start | bytes 104456 | tf_op jit(solution)/shard_map/ppermute | solution.py:38
  132.4 7.9 %copy-start.33 = (f32[256]{0:T(256)S(1)}, f32[256]{0:T(256)}, u32[]{:S(2)}) copy-start(f32[256]{0:T(256)} %param.23) | copy-start | bytes 3076
  132.4 5.7 %collective-permute-start.7 = (bf16[2,32,256]{2,1,0:T(8,128)(2,1)S(1)}, bf16[2,32,256]{2,1,0:T(8,128)(2,1)S(1)}, u32[]{:S(2)}, u32[]{:S(2)}) collective-permute-start(bf16[2,32,256]{2,1,0:T(8,128)(2,1)S(1)} %get-tuple-element.164), channel_id=1, source_target_pairs={{0,1},{1,2},{2,3},{4,5},{5,6},{6,7},{8,9},{9,10},{10,11},{12,13},{... | collective-permute-start | bytes 98312 | tf_op jit(solution)/shard_map/ppermute | solution.py:38
  135.0 5.2 %collective-permute-start.8 = (bf16[2,32,256]{2,1,0:T(8,128)(2,1)S(1)}, bf16[2,32,256]{2,1,0:T(8,128)(2,1)S(1)}, u32[]{:S(2)}, u32[]{:S(2)}) collective-permute-start(bf16[2,32,256]{2,1,0:T(8,128)(2,1)S(1)} %get-tuple-element.163), channel_id=1, source_target_pairs={{1,0},{2,1},{3,2},{5,4},{6,5},{7,6},{9,8},{10,9},{11,10},{13,12},{... | collective-permute-start | bytes 98312 | tf_op jit(solution)/shard_map/ppermute | solution.py:38
where the time goes:
time: 144 us; the launch traced here: 142 us
  local copies, waits for them, and re-layouts  54.6 us (38%)
  starting transfers between devices  24.5 us (17%)
  waiting for transfers between devices  22.4 us (16%)
  blocking collectives  18.9 us (13%)
  matrix products  10.9 us (8%)
  other arithmetic  9.37 us (7%)
    ppermute x5, waiting for transfers between devices, from_behind(): return lax.ppermute(array, axis, pairs)  22.2 us
    unnamed x89, local copies, waits for them, and re-layouts  17.8 us
    psum x1, blocking collectives, shards(): lax.psum((tile_sums, tile_squares), ('ha', 'wa'))  11.8 us
    slice x4, local copies, waits for them, and re-layouts, upsample_tile(): product[:, :, :, 2 * shift_row + shift_col]  11.6 us
    ppermute x5, starting transfers between devices, from_behind(): return lax.ppermute(array, axis, pairs)  10.4 us
    reshape x4, local copies, waits for them, and re-layouts, upsample_tile(): jnp.dot(flat, joined, preferred_element_type=jnp.float32)  8.62 us
    ppermute x2, starting transfers between devices, padded_2(): lax.ppermute(lax.slice_in_dim(block, 0, width, axis=dim), axis, backward)  8.17 us
    unnamed x1, blocking collectives  7.08 us
  transfers between devices with their start and end apart: 9, of which 4 were waited for; matrix products, arithmetic and copies ran while one was open for 8% of the time, Pallas kernels for 0%

commit v1 on v0

v1 whole, which is shorter than its diff:
```python
import functools

import jax
import jax.numpy as jnp
from jax import lax
from jax.experimental import pallas as pl
from jax.experimental.pallas import tpu as pltpu
from jax.sharding import PartitionSpec as P

GROUPS = 32
MESH = pl.DeviceIdType.MESH
DIRS = ((-1, 0), (1, 0), (0, -1), (0, 1), (-1, -1), (-1, 1), (1, -1), (1, 1))
KW_ORDER = (3, 1, 2, 0)


def section_kernel(
    n_tm, n_ha, n_wa,
    lat, gain, nbias, wconv_hbm, cbias, wup_hbm, ubias,
    out,
    wconv, wup, sums, plane_stats, block_stats,
    col_out, corner_out, row_in, col_in, corner_in, halo_norm, norm,
    acc0, acc1, part_out, part_in,
    feat, fcol_out, fcorner_out, frow_in, fcol_in, fcorner_in, fpad, spread,
    wsem, usem, pl_send, pl_recv, tm_send, tm_recv, h_send, h_recv, p_send, p_recv, f_send, f_recv,
):
    f32, bf16 = jnp.float32, jnp.bfloat16
    frames, height, breadth, chans = lat.shape
    couts = cbias.shape[-1]
    k, h, w = lax.axis_index("tm"), lax.axis_index("ha"), lax.axis_index("wa")
    n_plane = n_ha * n_wa
    me = h * n_wa + w

    conv_copies = [
        pltpu.make_async_copy(wconv_hbm.at[lag], wconv.at[lag], wsem.at[lag]) for lag in range(3)
    ]
    up_copies = [
        pltpu.make_async_copy(wup_hbm.at[:, kw], wup.at[:, slot], usem.at[slot])
        for slot, kw in enumerate(KW_ORDER)
    ]

    def plane_peer(d):
        q = lax.rem(me + d, n_plane)
        return q, (k, q // n_wa, lax.rem(q, n_wa))

    barrier = pltpu.get_barrier_semaphore()
    for d in range(1, n_plane):
        pl.semaphore_signal(barrier, inc=1, device_id=plane_peer(d)[1], device_id_type=MESH)
    for d in range(1, n_tm):
        pl.semaphore_signal(
            barrier, inc=1, device_id=(lax.rem(k + d, n_tm), h, w), device_id_type=MESH
        )
    for copy in conv_copies + up_copies:
        copy.start()

    def add_row(i, carry):
        total, square = carry
        t, r = i // height, lax.rem(i, height)
        row = lat[t, r].astype(f32)
        col_out[0, t, pl.ds(r, 1), :] = row[0:1]
        col_out[1, t, pl.ds(r, 1), :] = row[breadth - 1 : breadth]
        return total + row, square + row * row

    zero = jnp.zeros((breadth, chans), f32)
    total, square = lax.fori_loop(0, frames * height, add_row, (zero, zero), unroll=4)
    sums[0:1, :] = jnp.sum(total, axis=0, keepdims=True)
    sums[1:2, :] = jnp.sum(square, axis=0, keepdims=True)
    for i, (dy, dx) in enumerate(DIRS[4:]):
        r = 0 if dy < 0 else height - 1
        corner_out[i] = col_out[0 if dx < 0 else 1, :, r, :]
    pl.semaphore_wait(barrier, n_plane - 1 + n_tm - 1)

    def plane_copy(d, slot):
        q, where = plane_peer(d)
        index = me if slot is None else slot
        return pltpu.make_async_remote_copy(
            src_ref=sums, dst_ref=plane_stats.at[index], send_sem=pl_send.at[d],
            recv_sem=pl_recv.at[index], device_id=where, device_id_type=MESH,
        )

    for d in range(1, n_plane):
        plane_copy(d, None).start()
    plane_stats[me] = sums[...]

    def exists(dy, dx):
        ok = None
        for here, step, count in ((h, dy, n_ha), (w, dx, n_wa)):
            if step:
                one = (here + step >= 0) & (here + step < count)
                ok = one if ok is None else ok & one
        return ok

    def halo_copies(tile, cols, corners, rin, cin, kin, send, recv):
        made = []
        for i, (dy, dx) in enumerate(DIRS):
            if dx == 0:
                src, dst = tile.at[:, 0 if dy < 0 else height - 1], rin.at[1 if dy < 0 else 0]
            elif dy == 0:
                src, dst = cols.at[0 if dx < 0 else 1], cin.at[1 if dx < 0 else 0]
            else:
                src, dst = corners.at[i - 4], kin.at[7 - i]
            made.append((dy, dx, pltpu.make_async_remote_copy(
                src_ref=src, dst_ref=dst, send_sem=send.at[i], recv_sem=recv.at[i],
                device_id=(k, h + dy, w + dx), device_id_type=MESH,
            )))
        return made

    def start_all(made):
        for dy, dx, copy in made:
            pl.when(exists(dy, dx))(copy.start)

    def wait_send_all(made):
        for dy, dx, copy in made:
            pl.when(exists(dy, dx))(copy.wait_send)

    def wait_recv_all(made):
        for dy, dx, copy in made:
            pl.when(exists(-dy, -dx))(copy.wait_recv)

    halos = halo_copies(lat, col_out, corner_out, row_in, col_in, corner_in, h_send, h_recv)
    start_all(halos)

    for d in range(1, n_plane):
        plane_copy(d, plane_peer(d)[0]).wait_recv()
    block = plane_stats[0]
    for q in range(1, n_plane):
        block = block + plane_stats[q]
    block_stats[k] = block

    def tm_copy(d, slot):
        return pltpu.make_async_remote_copy(
            src_ref=block_stats.at[k], dst_ref=block_stats.at[slot], send_sem=tm_send.at[d],
            recv_sem=tm_recv.at[slot], device_id=(lax.rem(k + d, n_tm), h, w), device_id_type=MESH,
        )

    for d in range(1, n_tm):
        pl.when(k + d < n_tm)(tm_copy(d, k).start)
    wait_recv_all(halos)
    for d in range(1, n_tm):
        pl.when(k >= d)(tm_copy(d, lax.rem(k + n_tm - d, n_tm)).wait_recv)
    upto = block
    for q in range(n_tm):
        upto = upto + jnp.where(q < k, block_stats[q], 0.0)
    lane = lax.broadcasted_iota(jnp.int32, upto.shape, 1)
    group_width = chans // GROUPS
    step = 1
    while step < group_width:
        ahead = pltpu.roll(upto, chans - step, 1)
        behind = pltpu.roll(upto, step, 1)
        upto = upto + jnp.where((lane & step) == 0, ahead, behind)
        step *= 2
    cells = float(frames * height * breadth * n_plane * group_width)
    stats = upto / ((k + 1).astype(f32) * cells)
    mean = stats[0:1]
    variance = stats[1:2] - mean * mean
    half_scale = 0.5 * (lax.rsqrt(variance + 1e-06) * gain[...])
    half_bias = 0.5 * nbias[...]

    def normed(x):
        half = (x - mean) * half_scale + half_bias
        return half + half * jnp.tanh(half)

    up_ok, down_ok, left_ok, right_ok = exists(-1, 0), exists(1, 0), exists(0, -1), exists(0, 1)
    for side, ok in ((0, left_ok), (1, right_ok)):
        for t in range(frames):
            halo_norm[side, t, 1 : height + 1, :] = jnp.where(ok, normed(col_in[side, t]), 0.0)
    for i, (dy, dx) in enumerate(DIRS[4:]):
        row = 0 if dy < 0 else height + 1
        value = jnp.where(exists(dy, dx), normed(corner_in[i]), 0.0)
        for t in range(frames):
            halo_norm[0 if dx < 0 else 1, t, row : row + 1, :] = value[t : t + 1]

    def put_row(dest, t, r, y, left, right):
        column = lax.broadcasted_iota(jnp.int32, y.shape, 0)
        size = y.shape[1]
        dest[t, r, :, 0:size] = jnp.where(column == 0, left, pltpu.roll(y, 1, 0)).astype(bf16)
        dest[t, r, :, size : 2 * size] = y.astype(bf16)
        dest[t, r, :, 2 * size :] = jnp.where(
            column == breadth - 1, right, pltpu.roll(y, breadth - 1, 0)
        ).astype(bf16)

    def norm_row(i, carry):
        t, r = i // height, lax.rem(i, height)
        put_row(
            norm, t, r + 1, normed(lat[t, r].astype(f32)),
            halo_norm[0, t, pl.ds(r + 1, 1), :], halo_norm[1, t, pl.ds(r + 1, 1), :],
        )
        return carry

    lax.fori_loop(0, frames * height, norm_row, 0, unroll=2)
    for side, row, ok in ((0, 0, up_ok), (1, height + 1, down_ok)):
        for t in range(frames):
            put_row(
                norm, t, row, jnp.where(ok, normed(row_in[side, t].astype(f32)), 0.0),
                halo_norm[0, t, row : row + 1, :], halo_norm[1, t, row : row + 1, :],
            )

    cells_out = height * breadth

    def conv(first, last, lag):
        acc = None
        for dy in range(3):
            left = norm[first:last, dy : dy + height].reshape((last - first) * cells_out, 3 * chans)
            term = jnp.dot(
                left, wconv[lag, dy].reshape(3 * chans, couts), preferred_element_type=f32
            )
            acc = term if acc is None else acc + term
        return acc

    part = pltpu.make_async_remote_copy(
        src_ref=part_out, dst_ref=part_in, send_sem=p_send, recv_sem=p_recv,
        device_id=(lax.rem(k + 1, n_tm), h, w), device_id_type=MESH,
    )
    conv_copies[0].wait()
    lag0 = conv(0, 2, 0)
    acc0[...] = lag0[:cells_out]
    part_out[1] = lag0[cells_out:].astype(bf16)
    conv_copies[1].wait()
    part_out[0] = (acc0[...] + conv(1, 2, 1)).astype(bf16)
    pl.when(k + 1 < n_tm)(part.start)
    acc1[...] = conv(0, 1, 1)
    conv_copies[2].wait()
    lag2 = conv(0, 2, 2) + cbias[...]
    own0 = lag2[:cells_out]
    own1 = lag2[cells_out:] + acc1[...]
    pl.when(k > 0)(part.wait_recv)
    prior0 = jnp.where(k == 0, acc0[...] + acc1[...], part_in[0].astype(f32))
    prior1 = jnp.where(k == 0, acc0[...], part_in[1].astype(f32))
    feat[0] = (own0 + prior0).astype(bf16).reshape(height, breadth, couts)
    feat[1] = (own1 + prior1).astype(bf16).reshape(height, breadth, couts)

    def edge_row(i, carry):
        t, r = i // height, lax.rem(i, height)
        row = feat[t, r].astype(f32)
        fcol_out[0, t, pl.ds(r, 1), :] = row[0:1]
        fcol_out[1, t, pl.ds(r, 1), :] = row[breadth - 1 : breadth]
        return carry

    lax.fori_loop(0, frames * height, edge_row, 0, unroll=4)
    for i, (dy, dx) in enumerate(DIRS[4:]):
        r = 0 if dy < 0 else height - 1
        fcorner_out[i] = fcol_out[0 if dx < 0 else 1, :, r, :]
    fhalos = halo_copies(feat, fcol_out, fcorner_out, frow_in, fcol_in, fcorner_in, f_send, f_recv)
    start_all(fhalos)
    for copy in up_copies:
        copy.wait()
    wait_recv_all(fhalos)

    def feat_row(i, carry):
        t, r = i // height, lax.rem(i, height)
        put_row(
            fpad, t, r + 1, feat[t, r].astype(f32),
            jnp.where(left_ok, fcol_in[0, t, pl.ds(r, 1), :], 0.0),
            jnp.where(right_ok, fcol_in[1, t, pl.ds(r, 1), :], 0.0),
        )
        return carry

    lax.fori_loop(0, frames * height, feat_row, 0, unroll=2)
    for side, row, ok in ((0, 0, up_ok), (1, height + 1, down_ok)):
        for t in range(frames):
            put_row(
                fpad, t, row, jnp.where(ok, frow_in[side, t].astype(f32), 0.0),
                jnp.where(ok & left_ok, fcorner_in[2 * side, t : t + 1, :], 0.0),
                jnp.where(ok & right_ok, fcorner_in[2 * side + 1, t : t + 1, :], 0.0),
            )

    for row_par in (0, 1):
        for col_par in (0, 1):
            acc = None
            for off, kh in (((0, 3), (1, 1)) if row_par == 0 else ((1, 2), (2, 0))):
                left = fpad[:, off : off + height, :, col_par * couts : (col_par + 2) * couts]
                right = wup[kh, 2 * col_par : 2 * col_par + 2].reshape(2 * couts, couts)
                term = jnp.dot(
                    left.reshape(frames * cells_out, 2 * couts), right, preferred_element_type=f32
                )
                acc = term if acc is None else acc + term
            acc = (acc + ubias[...]).reshape(frames, height, breadth, couts)
            for t in range(frames):
                for half in range(couts // 128):
                    lanes = slice(half * 128, half * 128 + 128)
                    spread[half, t, :, row_par, pl.ds(col_par, breadth, stride=2), :] = acc[
                        t, :, :, lanes
                    ]
        for half in range(couts // 128):
            out[:, :, row_par, :, half * 128 : half * 128 + 128] = spread[half, :, :, row_par].astype(
                bf16
            )

    for d in range(1, n_plane):
        plane_copy(d, None).wait_send()
    for d in range(1, n_tm):
        pl.when(k + d < n_tm)(tm_copy(d, k).wait_send)
    wait_send_all(halos)
    pl.when(k + 1 < n_tm)(part.wait_send)
    wait_send_all(fhalos)


def shards(sizes, latent, norm_gain, norm_bias, conv_weight, conv_bias, up_weight, up_bias):
    n_tm, n_ha, n_wa = sizes
    frames, height, breadth, chans = latent.shape
    couts = conv_bias.shape[0]
    f32, bf16 = jnp.float32, jnp.bfloat16
    cells = height * breadth
    vmem = pl.BlockSpec(memory_space=pltpu.VMEM)
    hbm = pl.BlockSpec(memory_space=pl.ANY)
    dma = pltpu.SemaphoreType.DMA
    scratch = [
        pltpu.VMEM(conv_weight.shape, bf16),
        pltpu.VMEM(up_weight.shape, bf16),
        pltpu.VMEM((2, chans), f32),
        pltpu.VMEM((n_ha * n_wa, 2, chans), f32),
        pltpu.VMEM((n_tm, 2, chans), f32),
        pltpu.VMEM((2, frames, height, chans), f32),
        pltpu.VMEM((4, frames, chans), f32),
        pltpu.VMEM((2, frames, breadth, chans), bf16),
        pltpu.VMEM((2, frames, height, chans), f32),
        pltpu.VMEM((4, frames, chans), f32),
        pltpu.VMEM((2, frames, height + 2, chans), f32),
        pltpu.VMEM((frames, height + 2, breadth, 3 * chans), bf16),
        pltpu.VMEM((cells, couts), f32),
        pltpu.VMEM((cells, couts), f32),
        pltpu.VMEM((2, cells, couts), bf16),
        pltpu.VMEM((2, cells, couts), bf16),
        pltpu.VMEM((frames, height, breadth, couts), bf16),
        pltpu.VMEM((2, frames, height, couts), f32),
        pltpu.VMEM((4, frames, couts), f32),
        pltpu.VMEM((2, frames, breadth, couts), bf16),
        pltpu.VMEM((2, frames, height, couts), f32),
        pltpu.VMEM((4, frames, couts), f32),
        pltpu.VMEM((frames, height + 2, breadth, 3 * couts), bf16),
        pltpu.VMEM((couts // 128, frames, height, 2, 2 * breadth, 128), f32),
        dma((3,)), dma((4,)),
        dma((n_ha * n_wa,)), dma((n_ha * n_wa,)),
        dma((n_tm,)), dma((n_tm,)),
        dma((8,)), dma((8,)),
        dma(()), dma(()),
        dma((8,)), dma((8,)),
    ]
    result = pl.pallas_call(
        functools.partial(section_kernel, n_tm, n_ha, n_wa),
        out_shape=jax.ShapeDtypeStruct((frames, height, 2, 2 * breadth, couts), bf16),
        in_specs=[vmem, vmem, vmem, hbm, vmem, hbm, vmem],
        out_specs=vmem,
        scratch_shapes=scratch,
        compiler_params=pltpu.CompilerParams(
            collective_id=0, has_side_effects=True, vmem_limit_bytes=56 * 1024 * 1024
        ),
    )(
        latent, norm_gain[None], norm_bias[None], conv_weight, conv_bias[None], up_weight,
        up_bias[None],
    )
    return result.reshape(frames, 2 * height, 2 * breadth, couts)


def solution(mesh):
    sizes = (mesh.shape["tm"], mesh.shape["ha"], mesh.shape["wa"])
    in_specs = (P("tm", "ha", "wa", None), P(), P(), P(), P(), P(), P())
    out_specs = P("tm", "ha", "wa", None)
    return jax.shard_map(
        functools.partial(shards, sizes), mesh=mesh, in_specs=in_specs, out_specs=out_specs,
        check_vma=False,
    )
```

time: 144 us -> 31.8 us (0.22); the launches traced: 142 us -> 31.6 us
  local copies, waits for them, and re-layouts: 54.6 us -> 2.26 us
  Pallas kernels: 0 us -> 29.4 us
  starting transfers between devices: 24.5 us -> 0 us
  waiting for transfers between devices: 22.4 us -> 0 us
  blocking collectives: 18.9 us -> 0 us
  matrix products: 10.9 us -> 0 us
  other arithmetic: 9.37 us -> 0 us
    pallas_call x0 -> x1, Pallas kernels: none -> 29.4 us  [shards(): pl.pallas_call(functools.partial(section_kernel, n_tm, n_ha, n_wa), out_s...]
    ppermute x9 -> x0, starting transfers between devices: 24.5 us -> none  [the longest x5 10.4 us: from_behind(): return lax.ppermute(array, axis, pairs)]
    ppermute x9 -> x0, waiting for transfers between devices: 22.4 us -> none  [the longest x5 22.2 us: from_behind(): return lax.ppermute(array, axis, pairs)]
    slice x12 -> x0, local copies, waits for them, and re-layouts: 20.2 us -> none  [the longest x4 11.6 us: upsample_tile(): product[:, :, :, 2 * shift_row + shift_col]]
    unnamed x89 -> x1, local copies, waits for them, and re-layouts: 17.8 us -> 2.26 us
    psum x1 -> x0, blocking collectives: 11.8 us -> none  [shards(): lax.psum((tile_sums, tile_squares), ('ha', 'wa'))]
    dot_general x13 -> x0, matrix products: 10.9 us -> none  [the longest x4 5.78 us: upsample_tile(): jnp.dot(flat, joined, preferred_element_type=jnp.float32)]
    reshape x6 -> x0, local copies, waits for them, and re-layouts: 8.78 us -> none  [the longest x4 8.62 us: upsample_tile(): jnp.dot(flat, joined, preferred_element_type=jnp.float32)]
  transfers between devices with their start and end apart: 9 -> 0, of which waited for: 4 -> 0; matrix products, arithmetic and copies ran while one was open for 8% -> 0% of each run, Pallas kernels for 0% -> 0%
where the time goes in v1:
time: 31.8 us; the launch traced here: 31.6 us
  Pallas kernels  29.4 us (92%)
  local copies, waits for them, and re-layouts  2.26 us (7%)
    pallas_call x1, Pallas kernels, shards(): pl.pallas_call(functools.partial(section_kernel, n_tm, n_ha, n_wa), out_s...  29.4 us
    unnamed x1, local copies, waits for them, and re-layouts  2.26 us

profile of v1, /device:TPU:17, one launch (start us, length us, event | category | flops | bytes accessed | tf_op | source)
XLA Modules:
  0.0 31.6 jit_solution(12814569148393704175)
XLA Ops:
  0.0 29.4 %shard_map.73 = bf16[2,16,2,32,256]{4,3,2,1,0:T(8,128)(2,1)} custom-call(bf16[2,16,16,512]{3,2,1,0:T(8,128)(2,1)} %lat.1, f32[1,512]{1,0:T(1,128)} %bitcast.6, f32[1,512]{1,0:T(1,128)} %bitcast.7, bf16[3,3,3,512,256]{4,3,2,1,0:T(8,128)(2,1)} %wconv_hbm.1, f32[1,256]{1,0:T(1,128)} %bitcast.8, bf16[4,4,256,256]{3,2,1,0:T(8,128)(2,1)} %wup_hbm.1, f32[1,256]{1,0:T(1,128)} %bitcast.9), custom_call_target="tpu_custom_call" | custom-call | tf_op jit(solution)/shard_map/pallas_call | solution.py:338
  29.4 2.3 %copy.9 = bf16[2,32,32,256]{3,2,1,0:T(8,128)(2,1)} copy(bf16[2,32,32,256]{3,2,1,0:T(8,128)(2,1)} %bitcast.5) | data formatting | bytes 2097152

commit v2 on v1

--- a/solution.py
+++ b/solution.py
@@ -10,17 +10,16 @@
 GROUPS = 32
 MESH = pl.DeviceIdType.MESH
 DIRS = ((-1, 0), (1, 0), (0, -1), (0, 1), (-1, -1), (-1, 1), (1, -1), (1, 1))
-KW_ORDER = (3, 1, 2, 0)
 
 
 def section_kernel(
     n_tm, n_ha, n_wa,
-    lat, gain, nbias, wconv_hbm, cbias, wup_hbm, ubias,
-    out,
-    wconv, wup, sums, plane_stats, block_stats,
+    lat, gain, nbias, wconv_hbm, cbias, wup_hbm,
+    fpad, wup,
+    wconv, sums, plane_stats, block_stats,
     col_out, corner_out, row_in, col_in, corner_in, halo_norm, norm,
     acc0, acc1, part_out, part_in,
-    feat, fcol_out, fcorner_out, frow_in, fcol_in, fcorner_in, fpad, spread,
+    feat, fcol_out, fcorner_out, frow_in, fcol_in, fcorner_in,
     wsem, usem, pl_send, pl_recv, tm_send, tm_recv, h_send, h_recv, p_send, p_recv, f_send, f_recv,
 ):
     f32, bf16 = jnp.float32, jnp.bfloat16
@@ -33,10 +32,6 @@
     conv_copies = [
         pltpu.make_async_copy(wconv_hbm.at[lag], wconv.at[lag], wsem.at[lag]) for lag in range(3)
     ]
-    up_copies = [
-        pltpu.make_async_copy(wup_hbm.at[:, kw], wup.at[:, slot], usem.at[slot])
-        for slot, kw in enumerate(KW_ORDER)
-    ]
 
     def plane_peer(d):
         q = lax.rem(me + d, n_plane)
@@ -49,7 +44,8 @@
         pl.semaphore_signal(
             barrier, inc=1, device_id=(lax.rem(k + d, n_tm), h, w), device_id_type=MESH
         )
-    for copy in conv_copies + up_copies:
+    up_copy = pltpu.make_async_copy(wup_hbm, wup, usem)
+    for copy in conv_copies + [up_copy]:
         copy.start()
 
     def add_row(i, carry):
@@ -206,23 +202,29 @@
             acc = term if acc is None else acc + term
         return acc
 
-    part = pltpu.make_async_remote_copy(
-        src_ref=part_out, dst_ref=part_in, send_sem=p_send, recv_sem=p_recv,
-        device_id=(lax.rem(k + 1, n_tm), h, w), device_id_type=MESH,
-    )
+    parts = [
+        pltpu.make_async_remote_copy(
+            src_ref=part_out.at[i], dst_ref=part_in.at[i], send_sem=p_send.at[i],
+            recv_sem=p_recv.at[i], device_id=(lax.rem(k + 1, n_tm), h, w), device_id_type=MESH,
+        )
+        for i in range(2)
+    ]
     conv_copies[0].wait()
     lag0 = conv(0, 2, 0)
+    part_out[1] = lag0[cells_out:].astype(bf16)
+    pl.when(k + 1 < n_tm)(parts[1].start)
     acc0[...] = lag0[:cells_out]
-    part_out[1] = lag0[cells_out:].astype(bf16)
     conv_copies[1].wait()
-    part_out[0] = (acc0[...] + conv(1, 2, 1)).astype(bf16)
-    pl.when(k + 1 < n_tm)(part.start)
-    acc1[...] = conv(0, 1, 1)
+    lag1 = conv(0, 2, 1)
+    part_out[0] = (acc0[...] + lag1[cells_out:]).astype(bf16)
+    pl.when(k + 1 < n_tm)(parts[0].start)
+    acc1[...] = lag1[:cells_out]
     conv_copies[2].wait()
     lag2 = conv(0, 2, 2) + cbias[...]
     own0 = lag2[:cells_out]
     own1 = lag2[cells_out:] + acc1[...]
-    pl.when(k > 0)(part.wait_recv)
+    for part in parts:
+        pl.when(k > 0)(part.wait_recv)
     prior0 = jnp.where(k == 0, acc0[...] + acc1[...], part_in[0].astype(f32))
     prior1 = jnp.where(k == 0, acc0[...], part_in[1].astype(f32))
     feat[0] = (own0 + prior0).astype(bf16).reshape(height, breadth, couts)
@@ -241,20 +243,28 @@
         fcorner_out[i] = fcol_out[0 if dx < 0 else 1, :, r, :]
     fhalos = halo_copies(feat, fcol_out, fcorner_out, frow_in, fcol_in, fcorner_in, f_send, f_recv)
     start_all(fhalos)
-    for copy in up_copies:
-        copy.wait()
+
+    def feat_row(i, carry):
+        t, r = i // height, lax.rem(i, height)
+        put_row(fpad, t, r + 1, feat[t, r].astype(f32), 0.0, 0.0)
+        return carry
+
+    lax.fori_loop(0, frames * height, feat_row, 0, unroll=4)
     wait_recv_all(fhalos)
-
-    def feat_row(i, carry):
-        t, r = i // height, lax.rem(i, height)
-        put_row(
-            fpad, t, r + 1, feat[t, r].astype(f32),
-            jnp.where(left_ok, fcol_in[0, t, pl.ds(r, 1), :], 0.0),
-            jnp.where(right_ok, fcol_in[1, t, pl.ds(r, 1), :], 0.0),
-        )
+    column = lax.broadcasted_iota(jnp.int32, (breadth, couts), 0)
+
+    def edge_patch(i, carry):
+        t, r = i // height, lax.rem(i, height)
+        for side, ok, at in ((0, left_ok, 0), (1, right_ok, breadth - 1)):
+            lanes = slice(2 * side * couts, (2 * side + 1) * couts)
+            mixed = jnp.where(
+                (column == at) & ok, fcol_in[side, t, pl.ds(r, 1), :],
+                fpad[t, r + 1, :, lanes].astype(f32),
+            )
+            fpad[t, r + 1, :, lanes] = mixed.astype(bf16)
         return carry
 
-    lax.fori_loop(0, frames * height, feat_row, 0, unroll=2)
+    lax.fori_loop(0, frames * height, edge_patch, 0, unroll=4)
     for side, row, ok in ((0, 0, up_ok), (1, height + 1, down_ok)):
         for t in range(frames):
             put_row(
@@ -263,35 +273,48 @@
                 jnp.where(ok & right_ok, fcorner_in[2 * side + 1, t : t + 1, :], 0.0),
             )
 
+    up_copy.wait()
+    for d in range(1, n_plane):
+        plane_copy(d, None).wait_send()
+    for d in range(1, n_tm):
+        pl.when(k + d < n_tm)(tm_copy(d, k).wait_send)
+    wait_send_all(halos)
+    for part in parts:
+        pl.when(k + 1 < n_tm)(part.wait_send)
+    wait_send_all(fhalos)
+
+
+def upsample_kernel(fpad, wup, ubias, out, spread, ready, sem):
+    f32, bf16 = jnp.float32, jnp.bfloat16
+    frames, padded, breadth, _ = fpad.shape
+    height = padded - 2
+    couts = ubias.shape[-1]
+    copies = []
     for row_par in (0, 1):
         for col_par in (0, 1):
             acc = None
             for off, kh in (((0, 3), (1, 1)) if row_par == 0 else ((1, 2), (2, 0))):
                 left = fpad[:, off : off + height, :, col_par * couts : (col_par + 2) * couts]
-                right = wup[kh, 2 * col_par : 2 * col_par + 2].reshape(2 * couts, couts)
+                kws = (3, 1) if col_par == 0 else (2, 0)
+                right = jnp.concatenate([wup[kh, kw] for kw in kws], axis=0)
                 term = jnp.dot(
-                    left.reshape(frames * cells_out, 2 * couts), right, preferred_element_type=f32
+                    left.reshape(frames * height * breadth, 2 * couts), right,
+                    preferred_element_type=f32,
                 )
                 acc = term if acc is None else acc + term
             acc = (acc + ubias[...]).reshape(frames, height, breadth, couts)
-            for t in range(frames):
-                for half in range(couts // 128):
-                    lanes = slice(half * 128, half * 128 + 128)
-                    spread[half, t, :, row_par, pl.ds(col_par, breadth, stride=2), :] = acc[
-                        t, :, :, lanes
-                    ]
+            for half in range(couts // 128):
+                spread[half, :, :, row_par, pl.ds(col_par, breadth, stride=2), :] = acc[
+                    :, :, :, half * 128 : half * 128 + 128
+                ]
         for half in range(couts // 128):
-            out[:, :, row_par, :, half * 128 : half * 128 + 128] = spread[half, :, :, row_par].astype(
-                bf16
-            )
-
-    for d in range(1, n_plane):
-        plane_copy(d, None).wait_send()
-    for d in range(1, n_tm):
-        pl.when(k + d < n_tm)(tm_copy(d, k).wait_send)
-    wait_send_all(halos)
-    pl.when(k + 1 < n_tm)(part.wait_send)
-    wait_send_all(fhalos)
+            ready[row_par, :, :, :, half * 128 : half * 128 + 128] = spread[
+                half, :, :, row_par
+            ].astype(bf16)
+        copies.append(pltpu.make_async_copy(ready.at[row_par], out.at[:, :, row_par], sem.at[row_par]))
+        copies[-1].start()
+    for copy in copies:
+        copy.wait()
 
 
 def shards(sizes, latent, norm_gain, norm_bias, conv_weight, conv_bias, up_weight, up_bias):
@@ -305,7 +328,6 @@
     dma = pltpu.SemaphoreType.DMA
     scratch = [
         pltpu.VMEM(conv_weight.shape, bf16),
-        pltpu.VMEM(up_weight.shape, bf16),
         pltpu.VMEM((2, chans), f32),
         pltpu.VMEM((n_ha * n_wa, 2, chans), f32),
         pltpu.VMEM((n_tm, 2, chans), f32),
@@ -326,28 +348,38 @@
         pltpu.VMEM((2, frames, breadth, couts), bf16),
         pltpu.VMEM((2, frames, height, couts), f32),
         pltpu.VMEM((4, frames, couts), f32),
-        pltpu.VMEM((frames, height + 2, breadth, 3 * couts), bf16),
-        pltpu.VMEM((couts // 128, frames, height, 2, 2 * breadth, 128), f32),
-        dma((3,)), dma((4,)),
+        dma((3,)), dma(()),
         dma((n_ha * n_wa,)), dma((n_ha * n_wa,)),
         dma((n_tm,)), dma((n_tm,)),
         dma((8,)), dma((8,)),
-        dma(()), dma(()),
+        dma((2,)), dma((2,)),
         dma((8,)), dma((8,)),
     ]
-    result = pl.pallas_call(
+    fpad, wup = pl.pallas_call(
         functools.partial(section_kernel, n_tm, n_ha, n_wa),
-        out_shape=jax.ShapeDtypeStruct((frames, height, 2, 2 * breadth, couts), bf16),
-        in_specs=[vmem, vmem, vmem, hbm, vmem, hbm, vmem],
-        out_specs=vmem,
+        out_shape=[
+            jax.ShapeDtypeStruct((frames, height + 2, breadth, 3 * couts), bf16),
+            jax.ShapeDtypeStruct(up_weight.shape, bf16),
+        ],
+        in_specs=[vmem, vmem, vmem, pl.BlockSpec(memory_space=pltpu.HBM), vmem, pl.BlockSpec(memory_space=pltpu.HBM)],
+        out_specs=[vmem, vmem],
         scratch_shapes=scratch,
         compiler_params=pltpu.CompilerParams(
-            collective_id=0, has_side_effects=True, vmem_limit_bytes=56 * 1024 * 1024
+            collective_id=0, has_side_effects=True, vmem_limit_bytes=50 * 1024 * 1024
         ),
-    )(
-        latent, norm_gain[None], norm_bias[None], conv_weight, conv_bias[None], up_weight,
-        up_bias[None],
-    )
+    )(latent, norm_gain[None], norm_bias[None], conv_weight, conv_bias[None], up_weight)
+    result = pl.pallas_call(
+        upsample_kernel,
+        out_shape=jax.ShapeDtypeStruct((frames, height, 2, 2 * breadth, couts), bf16),
+        in_specs=[vmem, vmem, vmem],
+        out_specs=pl.BlockSpec(memory_space=pltpu.HBM),
+        scratch_shapes=[
+            pltpu.VMEM((couts // 128, frames, height, 2, 2 * breadth, 128), f32),
+            pltpu.VMEM((2, frames, height, 2 * breadth, couts), bf16),
+            dma((2,)),
+        ],
+        compiler_params=pltpu.CompilerParams(vmem_limit_bytes=20 * 1024 * 1024),
+    )(fpad, wup, up_bias[None])
     return result.reshape(frames, 2 * height, 2 * breadth, couts)
 
 

time: 31.8 us -> 27.9 us (0.88)
  Pallas kernels: 29.4 us -> 24.6 us
  local copies, waits for them, and re-layouts: 2.26 us -> 3.09 us
    pallas_call x1, Pallas kernels: 29.4 us -> 22.4 us  [shards(): pl.pallas_call(functools.partial(section_kernel, n_tm, n_ha, n_wa), out_s...]
    pallas_call x0 -> x1, Pallas kernels: none -> 2.22 us  [shards(): pl.pallas_call(upsample_kernel, out_shape=jax.ShapeDtypeStruct((frames, h...]
    unnamed x1 -> x10, local copies, waits for them, and re-layouts: 2.26 us -> 3.09 us
where the time goes in v2:
time: 27.9 us; the launch traced here: 27.7 us
  Pallas kernels  24.6 us (88%)
  local copies, waits for them, and re-layouts  3.09 us (11%)
    pallas_call x1, Pallas kernels, shards(): pl.pallas_call(functools.partial(section_kernel, n_tm, n_ha, n_wa), out_s...  22.4 us
    unnamed x10, local copies, waits for them, and re-layouts  3.09 us
    pallas_call x1, Pallas kernels, shards(): pl.pallas_call(upsample_kernel, out_shape=jax.ShapeDtypeStruct((frames, h...  2.22 us

profile of v2, /device:TPU:17, one launch (start us, length us, event | category | flops | bytes accessed | tf_op | source)
XLA Modules:
  0.0 27.7 jit_solution(14679708346746365970)
XLA Ops:
  0.0 0.0 copy-start
  0.0 1.0 %copy-done = bf16[2,16,16,512]{3,2,1,0:T(8,128)(2,1)S(1)} copy-done((bf16[2,16,16,512]{3,2,1,0:T(8,128)(2,1)S(1)}, bf16[2,16,16,512]{3,2,1,0:T(8,128)(2,1)}, u32[]{:S(2)}) %copy-start) | copy-done | bytes 524312
  1.0 0.0 copy-start.1
  1.0 0.7 %copy-done.1 = f32[512]{0:T(512)S(1)} copy-done((f32[512]{0:T(512)S(1)}, f32[512]{0:T(512)}, u32[]{:S(2)}) %copy-start.1) | copy-done | bytes 2072
  1.7 0.0 copy-start.2
  1.7 0.7 %copy-done.2 = f32[512]{0:T(512)S(1)} copy-done((f32[512]{0:T(512)S(1)}, f32[512]{0:T(512)}, u32[]{:S(2)}) %copy-start.2) | copy-done | bytes 2072
  2.4 0.0 copy-start.3
  2.4 0.7 %copy-done.3 = f32[256]{0:T(256)S(1)} copy-done((f32[256]{0:T(256)S(1)}, f32[256]{0:T(256)}, u32[]{:S(2)}) %copy-start.3) | copy-done | bytes 1048
  3.1 0.0 copy-start.4
  3.1 22.4 %shard_map.73 = (bf16[2,18,16,768]{3,2,1,0:T(8,128)(2,1)S(1)}, bf16[4,4,256,256]{3,2,1,0:T(8,128)(2,1)S(1)}) custom-call(bf16[2,16,16,512]{3,2,1,0:T(8,128)(2,1)S(1)} %copy-done, f32[1,512]{1,0:T(1,128)S(1)} %bitcast.5, f32[1,512]{1,0:T(1,128)S(1)} %bitcast.6, bf16[3,3,3,512,256]{4,3,2,1,0:T(8,128)(2,1)} %wconv_hbm.1, f32[1,256]{1,0:T(1,128)S(1)} %bitcast.7, ...), custom_call_target="tpu_custom_call" | custom-call | tf_op jit(solution)/shard_map/pallas_call | solution.py:358
  25.5 0.0 copy-done.4
  25.5 2.2 %shard_map.74 = bf16[2,16,2,32,256]{4,3,2,1,0:T(8,128)(2,1)} custom-call(bf16[2,18,16,768]{3,2,1,0:T(8,128)(2,1)S(1)} %get-tuple-element.7.fpad, bf16[4,4,256,256]{3,2,1,0:T(8,128)(2,1)S(1)} %get-tuple-element.8.wup, f32[1,256]{1,0:T(1,128)S(1)} %bitcast.8), custom_call_target="tpu_custom_call" | custom-call | tf_op jit(solution)/shard_map/pallas_call | solution.py:371
Async XLA Ops:
  0.0 1.0 %copy-start = (bf16[2,16,16,512]{3,2,1,0:T(8,128)(2,1)S(1)}, bf16[2,16,16,512]{3,2,1,0:T(8,128)(2,1)}, u32[]{:S(2)}) copy-start(bf16[2,16,16,512]{3,2,1,0:T(8,128)(2,1)} %lat.1) | copy-start | bytes 1572868
  1.0 0.7 %copy-start.1 = (f32[512]{0:T(512)S(1)}, f32[512]{0:T(512)}, u32[]{:S(2)}) copy-start(f32[512]{0:T(512)} %param.8) | copy-start | bytes 6148
  1.7 0.7 %copy-start.2 = (f32[512]{0:T(512)S(1)}, f32[512]{0:T(512)}, u32[]{:S(2)}) copy-start(f32[512]{0:T(512)} %param.9) | copy-start | bytes 6148
  2.4 0.7 %copy-start.3 = (f32[256]{0:T(256)S(1)}, f32[256]{0:T(256)}, u32[]{:S(2)}) copy-start(f32[256]{0:T(256)} %param.11) | copy-start | bytes 3076
  3.1 22.4 %copy-start.4 = (f32[256]{0:T(256)S(1)}, f32[256]{0:T(256)}, u32[]{:S(2)}) copy-start(f32[256]{0:T(256)} %param.13) | copy-start | bytes 3076

commit v3 on v2

--- a/solution.py
+++ b/solution.py
@@ -14,13 +14,13 @@
 
 def section_kernel(
     n_tm, n_ha, n_wa,
-    lat, gain, nbias, wconv_hbm, cbias, wup_hbm,
-    fpad, wup,
-    wconv, sums, plane_stats, block_stats,
+    lat_hbm, gain_hbm, nbias_hbm, wconv_hbm, cbias_hbm,
+    fpad,
+    lat, gain, nbias, cbias, wconv, sums, plane_stats, block_stats,
     col_out, corner_out, row_in, col_in, corner_in, halo_norm, norm,
     acc0, acc1, part_out, part_in,
     feat, fcol_out, fcorner_out, frow_in, fcol_in, fcorner_in,
-    wsem, usem, pl_send, pl_recv, tm_send, tm_recv, h_send, h_recv, p_send, p_recv, f_send, f_recv,
+    isem, wsem, pl_send, pl_recv, tm_send, tm_recv, h_send, h_recv, p_send, p_recv, f_send, f_recv,
 ):
     f32, bf16 = jnp.float32, jnp.bfloat16
     frames, height, breadth, chans = lat.shape
@@ -29,6 +29,14 @@
     n_plane = n_ha * n_wa
     me = h * n_wa + w
 
+    in_copies = [
+        pltpu.make_async_copy(source, held, isem.at[i])
+        for i, (source, held) in enumerate(
+            ((lat_hbm, lat), (gain_hbm, gain), (nbias_hbm, nbias), (cbias_hbm, cbias))
+        )
+    ]
+    for copy in in_copies:
+        copy.start()
     conv_copies = [
         pltpu.make_async_copy(wconv_hbm.at[lag], wconv.at[lag], wsem.at[lag]) for lag in range(3)
     ]
@@ -44,9 +52,11 @@
         pl.semaphore_signal(
             barrier, inc=1, device_id=(lax.rem(k + d, n_tm), h, w), device_id_type=MESH
         )
-    up_copy = pltpu.make_async_copy(wup_hbm, wup, usem)
-    for copy in conv_copies + [up_copy]:
+    for copy in conv_copies:
         copy.start()
+
+    for copy in in_copies:
+        copy.wait()
 
     def add_row(i, carry):
         total, square = carry
@@ -273,7 +283,6 @@
                 jnp.where(ok & right_ok, fcorner_in[2 * side + 1, t : t + 1, :], 0.0),
             )
 
-    up_copy.wait()
     for d in range(1, n_plane):
         plane_copy(d, None).wait_send()
     for d in range(1, n_tm):
@@ -327,6 +336,10 @@
     hbm = pl.BlockSpec(memory_space=pl.ANY)
     dma = pltpu.SemaphoreType.DMA
     scratch = [
+        pltpu.VMEM(latent.shape, bf16),
+        pltpu.VMEM((1, chans), f32),
+        pltpu.VMEM((1, chans), f32),
+        pltpu.VMEM((1, couts), f32),
         pltpu.VMEM(conv_weight.shape, bf16),
         pltpu.VMEM((2, chans), f32),
         pltpu.VMEM((n_ha * n_wa, 2, chans), f32),
@@ -348,26 +361,23 @@
         pltpu.VMEM((2, frames, breadth, couts), bf16),
         pltpu.VMEM((2, frames, height, couts), f32),
         pltpu.VMEM((4, frames, couts), f32),
-        dma((3,)), dma(()),
+        dma((4,)), dma((3,)),
         dma((n_ha * n_wa,)), dma((n_ha * n_wa,)),
         dma((n_tm,)), dma((n_tm,)),
         dma((8,)), dma((8,)),
         dma((2,)), dma((2,)),
         dma((8,)), dma((8,)),
     ]
-    fpad, wup = pl.pallas_call(
+    fpad = pl.pallas_call(
         functools.partial(section_kernel, n_tm, n_ha, n_wa),
-        out_shape=[
-            jax.ShapeDtypeStruct((frames, height + 2, breadth, 3 * couts), bf16),
-            jax.ShapeDtypeStruct(up_weight.shape, bf16),
-        ],
-        in_specs=[vmem, vmem, vmem, pl.BlockSpec(memory_space=pltpu.HBM), vmem, pl.BlockSpec(memory_space=pltpu.HBM)],
-        out_specs=[vmem, vmem],
+        out_shape=jax.ShapeDtypeStruct((frames, height + 2, breadth, 3 * couts), bf16),
+        in_specs=[pl.BlockSpec(memory_space=pltpu.HBM)] * 5,
+        out_specs=vmem,
         scratch_shapes=scratch,
         compiler_params=pltpu.CompilerParams(
-            collective_id=0, has_side_effects=True, vmem_limit_bytes=50 * 1024 * 1024
+            collective_id=0, has_side_effects=True, vmem_limit_bytes=57 * 1024 * 1024
         ),
-    )(latent, norm_gain[None], norm_bias[None], conv_weight, conv_bias[None], up_weight)
+    )(latent, norm_gain[None], norm_bias[None], conv_weight, conv_bias[None])
     result = pl.pallas_call(
         upsample_kernel,
         out_shape=jax.ShapeDtypeStruct((frames, height, 2, 2 * breadth, couts), bf16),
@@ -379,7 +389,7 @@
             dma((2,)),
         ],
         compiler_params=pltpu.CompilerParams(vmem_limit_bytes=20 * 1024 * 1024),
-    )(fpad, wup, up_bias[None])
+    )(fpad, up_weight, up_bias[None])
     return result.reshape(frames, 2 * height, 2 * breadth, couts)
 
 

time: 27.9 us -> 27 us (0.968)
  local copies, waits for them, and re-layouts: 3.09 us -> 1.17 us
  Pallas kernels: 24.6 us -> 25.6 us
    unnamed x10 -> x6, local copies, waits for them, and re-layouts: 3.09 us -> 1.17 us
    pallas_call x1, Pallas kernels: 22.4 us -> 23.4 us  [shards(): pl.pallas_call(functools.partial(section_kernel, n_tm, n_ha, n_wa), out_s...]
where the time goes in v3:
time: 27 us; the launch traced here: 26.8 us
  Pallas kernels  25.6 us (95%)
  local copies, waits for them, and re-layouts  1.17 us (4%)
    pallas_call x1, Pallas kernels, shards(): pl.pallas_call(functools.partial(section_kernel, n_tm, n_ha, n_wa), out_s...  23.4 us
    pallas_call x1, Pallas kernels, shards(): pl.pallas_call(upsample_kernel, out_shape=jax.ShapeDtypeStruct((frames, h...  2.21 us
    unnamed x6, local copies, waits for them, and re-layouts  1.17 us

profile of v3, /device:TPU:17, one launch (start us, length us, event | category | flops | bytes accessed | tf_op | source)
XLA Modules:
  0.0 26.8 jit_solution(661423893152676675)
XLA Ops:
  0.0 0.0 copy-start.2
  0.0 0.0 copy-start.1
  0.0 23.4 %shard_map.73.fpad = bf16[2,18,16,768]{3,2,1,0:T(8,128)(2,1)} custom-call(bf16[2,16,16,512]{3,2,1,0:T(8,128)(2,1)} %lat_hbm.1, f32[1,512]{1,0:T(1,128)} %bitcast.6, f32[1,512]{1,0:T(1,128)} %bitcast.7, bf16[3,3,3,512,256]{4,3,2,1,0:T(8,128)(2,1)} %wconv_hbm.1, f32[1,256]{1,0:T(1,128)} %bitcast.8), custom_call_target="tpu_custom_call" | custom-call | tf_op jit(solution)/shard_map/pallas_call | solution.py:371
  23.4 0.0 copy-done.2
  23.4 0.0 copy-done.1
  23.4 0.0 copy-start
  23.5 1.2 %copy-done = bf16[2,18,16,768]{3,2,1,0:T(8,128)(2,1)S(1)} copy-done((bf16[2,18,16,768]{3,2,1,0:T(8,128)(2,1)S(1)}, bf16[2,18,16,768]{3,2,1,0:T(8,128)(2,1)}, u32[]{:S(2)}) %copy-start) | copy-done | bytes 884760
  24.6 2.2 %shard_map.74 = bf16[2,16,2,32,256]{4,3,2,1,0:T(8,128)(2,1)} custom-call(bf16[2,18,16,768]{3,2,1,0:T(8,128)(2,1)S(1)} %copy-done, bf16[4,4,256,256]{3,2,1,0:T(8,128)(2,1)S(1)} %copy-done.1, f32[1,256]{1,0:T(1,128)S(1)} %bitcast.5), custom_call_target="tpu_custom_call" | custom-call | tf_op jit(solution)/shard_map/pallas_call | solution.py:381
Async XLA Ops:
  0.0 23.4 %copy-start.2 = (f32[256]{0:T(256)S(1)}, f32[256]{0:T(256)}, u32[]{:S(2)}) copy-start(f32[256]{0:T(256)} %param.13) | copy-start | bytes 3076
  0.0 23.4 %copy-start.1 = (bf16[4,4,256,256]{3,2,1,0:T(8,128)(2,1)S(1)}, bf16[4,4,256,256]{3,2,1,0:T(8,128)(2,1)}, u32[]{:S(2)}) copy-start(bf16[4,4,256,256]{3,2,1,0:T(8,128)(2,1)} %wup.1) | copy-start | bytes 6291460
  23.4 1.2 %copy-start = (bf16[2,18,16,768]{3,2,1,0:T(8,128)(2,1)S(1)}, bf16[2,18,16,768]{3,2,1,0:T(8,128)(2,1)}, u32[]{:S(2)}) copy-start(bf16[2,18,16,768]{3,2,1,0:T(8,128)(2,1)} %shard_map.73.fpad) | copy-start | bytes 2654212
